TPU v7x, 256 devices: a whole 4x4x8 slice. The times are simulated.
256 devices in a mesh: dp: 8 (over y, core), expert: 32 (over x, z).
Axes of the slice: x: 4, y: 4, z: 8, core: 2. Of those that a mesh axis runs over, the one named last changes fastest.
Arguments:
- tokens: bfloat16 [8192, 2048], P(('dp', 'expert')), may hold values from -6 to 6
- expert_ids: int32 [8192, 8], P(('dp', 'expert')), may hold values from 0 to 31, all different within a row; in each aligned block of 32 rows (0 to 31, 32 to 63, ...) at most 12 rows name the same one
- gate_weights: float32 [8192, 8], P(('dp', 'expert')), may hold values from 0.05 to 0.5
- cotangent: bfloat16 [8192, 2048], P(('dp', 'expert')), may hold values from -6 to 6
- w_gate: bfloat16 [32, 1536, 2048], P('expert', 'dp'), may hold values from -0.125 to 0.125
- w_up: bfloat16 [32, 1536, 2048], P('expert', 'dp'), may hold values from -0.125 to 0.125
- w_down: bfloat16 [32, 1536, 2048], P('expert', 'dp'), may hold values from -0.15625 to 0.15625
Outputs:
- layer_out: bfloat16 [8192, 2048], P(('dp', 'expert'))
- input_grad: bfloat16 [8192, 2048], P(('dp', 'expert'))
Inputs may be any that keep to these rules, and one draw needn't show every extreme that they name: `expert_ids`: each row names 8 different experts. Among the 32 rows of one device (aligned blocks of rows), no expert is named by more than 12 rows, and in every draw some expert is named by exactly 12 rows of some device.
All inputs are finite; a program needn't handle non-finite values.
Results may differ from a plain program's by a relative error of at most 0.011.
Values may be sent and summed in bfloat16 or wider, within the bound.
A program may use at most 128 MiB of HBM per device.

v0:
```python
import jax
import jax.numpy as jnp
from jax import lax
from jax.sharding import PartitionSpec as P


def expert_terms(rows_in, rows_back, gate_mat, up_mat, down_mat):
    pre_gate = jnp.einsum("secd,ehd->sech", rows_in, gate_mat, preferred_element_type=jnp.float32)
    pre_up = jnp.einsum("secd,ehd->sech", rows_in, up_mat, preferred_element_type=jnp.float32)
    sig_gate = jax.nn.sigmoid(pre_gate)
    silu_gate = pre_gate * sig_gate
    hidden = (silu_gate * pre_up).astype(jnp.bfloat16)
    expert_out = jnp.einsum("sech,ehd->secd", hidden, down_mat, preferred_element_type=jnp.float32)
    back_term = jnp.einsum(
        "secd,ehd->sech", rows_back, down_mat, preferred_element_type=jnp.float32
    )
    grad_gate = (back_term * pre_up * sig_gate * (1.0 + pre_gate * (1.0 - sig_gate))).astype(
        jnp.bfloat16
    )
    grad_up = (back_term * silu_gate).astype(jnp.bfloat16)
    slot_grad = jnp.einsum(
        "sech,ehd->secd", grad_gate, gate_mat, preferred_element_type=jnp.float32
    )
    slot_grad = slot_grad + jnp.einsum(
        "sech,ehd->secd", grad_up, up_mat, preferred_element_type=jnp.float32
    )
    return (expert_out, slot_grad)


def shards(tokens, expert_ids, gate_weights, cotangent, w_gate, w_up, w_down):
    tok_rows, width = tokens.shape
    top_count = expert_ids.shape[1]
    expert_devs = lax.axis_size("expert")
    local_count = w_gate.shape[0]
    experts_all = local_count * expert_devs
    capacity = min(tok_rows, (3 * tok_rows * top_count + 2 * experts_all - 1) // (2 * experts_all))
    flat_ids = expert_ids.reshape(-1)
    onehot = (flat_ids[:, None] == jnp.arange(experts_all, dtype=jnp.int32)[None, :]).astype(
        jnp.int32
    )
    slot_rank = jnp.sum((jnp.cumsum(onehot, axis=0) - onehot) * onehot, axis=1)
    slot_index = flat_ids * capacity + slot_rank
    token_of = jnp.arange(tok_rows * top_count, dtype=jnp.int32) // top_count
    slot_owner = (
        jnp.full((experts_all * capacity,), tok_rows, jnp.int32).at[slot_index].set(token_of)
    )
    padded_in = jnp.concatenate([tokens, jnp.zeros((1, width), tokens.dtype)], axis=0)
    padded_back = jnp.concatenate([cotangent, jnp.zeros((1, width), cotangent.dtype)], axis=0)
    send_in = padded_in[slot_owner].reshape(expert_devs, local_count * capacity, width)
    send_back = padded_back[slot_owner].reshape(expert_devs, local_count * capacity, width)
    recv_in, recv_back = (
        lax.all_to_all(send_in, "expert", split_axis=0, concat_axis=0, tiled=True),
        lax.all_to_all(send_back, "expert", split_axis=0, concat_axis=0, tiled=True),
    )
    rows_in = recv_in.reshape(expert_devs, local_count, capacity, width)
    rows_back = recv_back.reshape(expert_devs, local_count, capacity, width)
    gate_mat, up_mat, down_mat = (
        lax.all_gather(w_gate, "dp", axis=1, tiled=True),
        lax.all_gather(w_up, "dp", axis=1, tiled=True),
        lax.all_gather(w_down, "dp", axis=1, tiled=True),
    )
    out_sum, grad_sum = expert_terms(rows_in, rows_back, gate_mat, up_mat, down_mat)
    out_send = out_sum.astype(jnp.bfloat16).reshape(expert_devs, local_count * capacity, width)
    grad_send = grad_sum.astype(jnp.bfloat16).reshape(expert_devs, local_count * capacity, width)
    back_out, back_grad = (
        lax.all_to_all(out_send, "expert", split_axis=0, concat_axis=0, tiled=True),
        lax.all_to_all(grad_send, "expert", split_axis=0, concat_axis=0, tiled=True),
    )
    picked_out = back_out.reshape(experts_all * capacity, width)[slot_index]
    picked_grad = back_grad.reshape(experts_all * capacity, width)[slot_index]
    picked_out = picked_out.reshape(tok_rows, top_count, width).astype(jnp.float32)
    picked_grad = picked_grad.reshape(tok_rows, top_count, width).astype(jnp.float32)
    layer_out = jnp.einsum("tk,tkd->td", gate_weights, picked_out)
    input_grad = jnp.einsum("tk,tkd->td", gate_weights, picked_grad)
    return (layer_out.astype(jnp.bfloat16), input_grad.astype(jnp.bfloat16))


def solution(mesh):
    return jax.shard_map(
        shards,
        mesh=mesh,
        in_specs=(
            P(("dp", "expert"), None),
            P(("dp", "expert"), None),
            P(("dp", "expert"), None),
            P(("dp", "expert"), None),
            P("expert", "dp", None),
            P("expert", "dp", None),
            P("expert", "dp", None),
        ),
        out_specs=(P(("dp", "expert"), None), P(("dp", "expert"), None)),
        check_vma=False,
    )
```

profile of v0, /device:TPU:64, one launch (start us, length us, event | category | flops | bytes accessed | tf_op | source)
XLA Modules:
  0.0 293.1 jit_solution(12005172879646309945)
XLA Ops:
  7.2 0.0 all-gather.4.cloned.1.call-start
  7.2 0.7 all-gather.4.cloned.1.call-update
  7.9 0.0 all-gather.6.cloned.1.call-start
  8.0 0.7 all-gather.6.cloned.1.call-update
  8.7 0.0 all-gather.8.cloned.1.call-start
  8.7 0.7 all-gather.8.cloned.1.call-update
  9.4 0.0 copy-done.3
  9.4 0.1 copy.18
  9.5 0.1 eq.29
  9.6 0.1 eq.25
  9.7 0.1 copy.17
  9.8 0.1 mul.42
  9.9 0.6 reduce-window.6
  10.5 0.2 slice_reduce_fusion
  10.7 0.1 fusion.43
  10.8 1.4 scatter_custom_fusion
  12.3 2.5 gather_fusion
  14.7 1.5 reshape.109
  16.2 10.9 %all-to-all-start = ((bf16[32,12,2048]{2,1,0:T(8,128)(2,1)}), bf16[32,12,2048]{2,1,0:T(8,128)(2,1)}, u32[]{:S(2)}, u32[]{:S(2)}) async-start(bf16[32,12,2048]{2,1,0:T(8,128)(2,1)} %reshape.109), calls=%async_computation | async-start | bytes 4194304 | tf_op jit(solution)/shard_map/all_to_all | solution.py:52
  27.2 2.5 gather_fusion.2
  29.7 1.5 reshape.116
  31.2 46.1 %all-to-all-done = bf16[32,12,2048]{2,1,0:T(8,128)(2,1)} async-done(((bf16[32,12,2048]{2,1,0:T(8,128)(2,1)}), bf16[32,12,2048]{2,1,0:T(8,128)(2,1)}, u32[]{:S(2)}, u32[]{:S(2)}) %all-to-all-start) | async-done | bytes 1572896 | tf_op jit(solution)/shard_map/all_to_all | solution.py:52
  77.3 6.2 %all-to-all-start.2 = ((bf16[32,12,2048]{2,1,0:T(8,128)(2,1)}), bf16[32,12,2048]{2,1,0:T(8,128)(2,1)S(1)}, u32[]{:S(2)}, u32[]{:S(2)}) async-start(bf16[32,12,2048]{2,1,0:T(8,128)(2,1)} %reshape.116), calls=%async_computation.2 | async-start | bytes 4194304 | tf_op jit(solution)/shard_map/all_to_all | solution.py:53
  83.4 0.0 all-gather.4.cloned.1.call-done
  83.4 8.3 %fusion.12 = f32[32,1,12,1536]{3,0,2,1:T(8,128)} fusion(bf16[1,1536,2048]{2,1,0:T(8,128)(2,1)} %all-gather.4.cloned.1.call-done, bf16[32,12,2048]{2,1,0:T(8,128)(2,1)} %all-to-all-done), kind=kOutput, calls=%fused_computation.18 | convolution fusion | flops 2415919104 | bytes 10223616 | tf_op jit(solution)/shard_map/secd,ehd->sech/dot_general | solution.py:8
  91.8 9.3 %all-gather.6.cloned.1.call-done = bf16[1,1536,2048]{2,1,0:T(8,128)(2,1)} async-done(((bf16[1,192,2048]{2,1,0:T(8,128)(2,1)}), bf16[1,1536,2048]{2,1,0:T(8,128)(2,1)}) %all-gather.6.cloned.1.call-update) | async-done | bytes 6291472 | tf_op jit(solution)/shard_map/all_gather | solution.py:59
  101.1 8.2 %fusion.15 = f32[32,1,12,1536]{3,0,2,1:T(8,128)} fusion(bf16[1,1536,2048]{2,1,0:T(8,128)(2,1)} %all-gather.6.cloned.1.call-done, bf16[32,12,2048]{2,1,0:T(8,128)(2,1)} %all-to-all-done), kind=kOutput, calls=%fused_computation.19 | convolution fusion | flops 2415919104 | bytes 10223616 | tf_op jit(solution)/shard_map/secd,ehd->sech/dot_general | solution.py:9
  109.3 23.9 %all-to-all-done.2 = bf16[32,12,2048]{2,1,0:T(8,128)(2,1)S(1)} async-done(((bf16[32,12,2048]{2,1,0:T(8,128)(2,1)}), bf16[32,12,2048]{2,1,0:T(8,128)(2,1)S(1)}, u32[]{:S(2)}, u32[]{:S(2)}) %all-to-all-start.2) | async-done | bytes 1572896 | tf_op jit(solution)/shard_map/all_to_all | solution.py:53
  133.2 13.3 %all-gather.8.cloned.1.call-done = bf16[1,1536,2048]{2,1,0:T(8,128)(2,1)} async-done(((bf16[1,192,2048]{2,1,0:T(8,128)(2,1)}), bf16[1,1536,2048]{2,1,0:T(8,128)(2,1)}) %all-gather.8.cloned.1.call-update) | async-done | bytes 6291472 | tf_op jit(solution)/shard_map/all_gather | solution.py:60
  146.5 7.0 %fusion.18 = f32[32,1,12,1536]{3,0,2,1:T(8,128)S(1)} fusion(bf16[1,1536,2048]{2,1,0:T(8,128)(2,1)} %all-gather.8.cloned.1.call-done, bf16[32,12,2048]{2,1,0:T(8,128)(2,1)S(1)} %all-to-all-done.2), kind=kOutput, calls=%fused_computation.20 | convolution fusion | flops 2415919104 | bytes 10223616 | tf_op jit(solution)/shard_map/secd,ehd->sech/dot_general | solution.py:14
  153.5 0.0 slice-start.1
  153.5 2.7 fusion.4
  156.3 3.3 %add_convert_fusion = bf16[32,12,2048]{2,0,1:T(8,128)(2,1)S(1)} fusion(f32[32,12,2048]{2,0,1:T(8,128)S(1)} %fusion.4, bf16[1,1536,2048]{2,1,0:T(8,128)(2,1)S(1)} %bitcast.95, f32[32,1,12,1536]{3,0,2,1:T(8,128)S(1)} %copy-done.6, f32[32,1,12,1536]{3,0,2,1:T(8,128)S(1)} %fusion.18, f32[32,1,12,1536]{3,0,2,1:T(8,128)S(1)} %copy-done.7), kind=kOutput, calls=%fused_computation.17 | convolution fusion | flops 2423390208 | bytes 18087936 | tf_op jit(solution)/shard_map/sech,ehd->secd/dot_general | solution.py:21
  159.6 2.2 copy.25
  161.8 10.0 %all-to-all-start.3 = ((bf16[32,12,2048]{2,1,0:T(8,128)(2,1)}), bf16[32,12,2048]{2,1,0:T(8,128)(2,1)S(1)}, u32[]{:S(2)}, u32[]{:S(2)}) async-start(bf16[32,12,2048]{2,1,0:T(8,128)(2,1)} %copy.25), calls=%async_computation.3 | async-start | bytes 4194304 | tf_op jit(solution)/shard_map/all_to_all | solution.py:67
  171.8 6.9 %fusion.23 = bf16[32,12,2048]{2,0,1:T(8,128)(2,1)S(1)} fusion(bf16[1,1536,2048]{2,1,0:T(8,128)(2,1)} %all-gather.8.cloned.1.call-done, f32[32,1,12,1536]{3,0,2,1:T(8,128)} %fusion.15, f32[32,1,12,1536]{3,0,2,1:T(8,128)} %fusion.12), kind=kOutput, calls=%fused_computation.21 | convolution fusion | flops 2420244480 | bytes 12582912 | tf_op jit(solution)/shard_map/sech,ehd->secd/dot_general | solution.py:13
  178.7 2.2 copy.23
  180.9 41.4 %all-to-all-done.3 = bf16[32,12,2048]{2,1,0:T(8,128)(2,1)S(1)} async-done(((bf16[32,12,2048]{2,1,0:T(8,128)(2,1)}), bf16[32,12,2048]{2,1,0:T(8,128)(2,1)S(1)}, u32[]{:S(2)}, u32[]{:S(2)}) %all-to-all-start.3) | async-done | bytes 1572896 | tf_op jit(solution)/shard_map/all_to_all | solution.py:67
  222.3 6.4 %all-to-all-start.1 = ((bf16[32,12,2048]{2,1,0:T(8,128)(2,1)}), bf16[32,12,2048]{2,1,0:T(8,128)(2,1)}, u32[]{:S(2)}, u32[]{:S(2)}) async-start(bf16[32,12,2048]{2,1,0:T(8,128)(2,1)} %copy.23), calls=%async_computation.1 | async-start | bytes 4194304 | tf_op jit(solution)/shard_map/all_to_all | solution.py:66
  228.7 0.1 copy.26
  228.8 2.5 reshape.119
  231.4 1.4 gather_fusion.3
  232.7 46.1 %all-to-all-done.1 = bf16[32,12,2048]{2,1,0:T(8,128)(2,1)} async-done(((bf16[32,12,2048]{2,1,0:T(8,128)(2,1)}), bf16[32,12,2048]{2,1,0:T(8,128)(2,1)}, u32[]{:S(2)}, u32[]{:S(2)}) %all-to-all-start.1) | async-done | bytes 1572896 | tf_op jit(solution)/shard_map/all_to_all | solution.py:66
  278.8 2.5 reshape.114
  281.3 2.3 gather_fusion.1
  283.7 0.4 fusion.35
  284.1 1.6 fusion.37
  285.8 0.8 bitcast_convert_fusion
  (30 shorter events, 0.1 us)
Async XLA Ops:
  7.2 2.2 copy-start.3
  7.2 3.5 %copy-start.1 = (bf16[32,2048]{1,0:T(8,128)(2,1)S(1)}, bf16[32,2048]{1,0:T(8,128)(2,1)}, u32[]{:S(2)}) copy-start(bf16[32,2048]{1,0:T(8,128)(2,1)} %param.7) | copy-start | bytes 393220
  7.2 76.3 %all-gather.4.cloned.1.call-start = ((), (), s32[]{:S(2)}) async-start(), calls=%async_computation.4 | async-start | bytes 7077888 | tf_op jit(solution)/shard_map/all_gather | solution.py:58
  7.9 93.1 %all-gather.6.cloned.1.call-start = ((), (), s32[]{:S(2)}) async-start(), calls=%async_computation.5 | async-start | bytes 7077888 | tf_op jit(solution)/shard_map/all_gather | solution.py:59
  8.7 137.8 %all-gather.8.cloned.1.call-start = ((), (), s32[]{:S(2)}) async-start(), calls=%async_computation.6 | async-start | bytes 7077888 | tf_op jit(solution)/shard_map/all_gather | solution.py:60
  16.2 10.9 %copy-start.2 = (bf16[32,2048]{1,0:T(8,128)(2,1)S(1)}, bf16[32,2048]{1,0:T(8,128)(2,1)}, u32[]{:S(2)}) copy-start(bf16[32,2048]{1,0:T(8,128)(2,1)} %param.10) | copy-start | bytes 393220
  16.2 61.0 %all-to-all-start = ((bf16[32,12,2048]{2,1,0:T(8,128)(2,1)}), bf16[32,12,2048]{2,1,0:T(8,128)(2,1)}, u32[]{:S(2)}, u32[]{:S(2)}) async-start(bf16[32,12,2048]{2,1,0:T(8,128)(2,1)} %reshape.109), calls=%async_computation | async-start | bytes 4194304 | tf_op jit(solution)/shard_map/all_to_all | solution.py:52
  77.3 55.9 %all-to-all-start.2 = ((bf16[32,12,2048]{2,1,0:T(8,128)(2,1)}), bf16[32,12,2048]{2,1,0:T(8,128)(2,1)S(1)}, u32[]{:S(2)}, u32[]{:S(2)}) async-start(bf16[32,12,2048]{2,1,0:T(8,128)(2,1)} %reshape.116), calls=%async_computation.2 | async-start | bytes 4194304 | tf_op jit(solution)/shard_map/all_to_all | solution.py:53
  146.5 7.0 %copy-start.5 = (bf16[1,1536,2048]{2,1,0:T(8,128)(2,1)S(1)}, bf16[1,1536,2048]{2,1,0:T(8,128)(2,1)}, u32[]{:S(2)}) copy-start(bf16[1,1536,2048]{2,1,0:T(8,128)(2,1)} %all-gather.6.cloned.1.call-done) | copy-start | bytes 18874372
  146.5 7.0 %copy-start.6 = (f32[32,1,12,1536]{3,0,2,1:T(8,128)S(1)}, f32[32,1,12,1536]{3,0,2,1:T(8,128)}, u32[]{:S(2)}) copy-start(f32[32,1,12,1536]{3,0,2,1:T(8,128)} %fusion.12) | copy-start | bytes 7077892
  146.5 9.7 %slice-start = ((s8[6291456]{0:T(1024)(128)(4,1)}), s8[4194304]{0:T(1024)(128)(4,1)S(1)}, s32[]{:S(2)}) async-start(s8[6291456]{0:T(1024)(128)(4,1)} %bitcast.94), calls=%async_computation.7 | async-start | bytes 8388608
  153.5 2.8 slice-start.1
  153.5 2.8 copy-start.7
  161.8 60.5 %all-to-all-start.3 = ((bf16[32,12,2048]{2,1,0:T(8,128)(2,1)}), bf16[32,12,2048]{2,1,0:T(8,128)(2,1)S(1)}, u32[]{:S(2)}, u32[]{:S(2)}) async-start(bf16[32,12,2048]{2,1,0:T(8,128)(2,1)} %copy.25), calls=%async_computation.3 | async-start | bytes 4194304 | tf_op jit(solution)/shard_map/all_to_all | solution.py:67
  180.9 47.8 %copy-start.4 = (f32[32,8]{0,1:T(8,128)S(1)}, f32[32,8]{0,1:T(8,128)}, u32[]{:S(2)}) copy-start(f32[32,8]{0,1:T(8,128)} %param.9) | copy-start | bytes 3076
  222.3 6.5 %copy-start = (bf16[32,12,2048]{2,1,0:T(8,128)(2,1)}, bf16[32,12,2048]{2,1,0:T(8,128)(2,1)S(1)}, u32[]{:S(2)}) copy-start(bf16[32,12,2048]{2,1,0:T(8,128)(2,1)S(1)} %all-to-all-done.3) | copy-start | bytes 4718596
  222.3 56.6 %all-to-all-start.1 = ((bf16[32,12,2048]{2,1,0:T(8,128)(2,1)}), bf16[32,12,2048]{2,1,0:T(8,128)(2,1)}, u32[]{:S(2)}, u32[]{:S(2)}) async-start(bf16[32,12,2048]{2,1,0:T(8,128)(2,1)} %copy.23), calls=%async_computation.1 | async-start | bytes 4194304 | tf_op jit(solution)/shard_map/all_to_all | solution.py:66
Sparse Core Ops, SparseCore 0:
  9.8 45.7 all-gather.3
  57.5 43.5 all-gather.5
  102.9 43.5 all-gather.7
where the time goes:
time: 294 us; the launch traced here: 293 us
  waiting for transfers between devices  182 us (62%)
  matrix products  38.4 us (13%)
  starting transfers between devices  33.6 us (11%)
  local copies, waits for them, and re-layouts  24.1 us (8%)
  between operations  14.1 us (5%)
    all_to_all x1, waiting for transfers between devices, shards(): lax.all_to_all(out_send, 'expert', split_axis=0, concat_axis=0, tiled=True)  46.1 us
    all_to_all x1, waiting for transfers between devices, shards(): lax.all_to_all(send_in, 'expert', split_axis=0, concat_axis=0, tiled=True)  46.1 us
    all_to_all x1, waiting for transfers between devices, shards(): lax.all_to_all(grad_send, 'expert', split_axis=0, concat_axis=0, tiled=True)  41.4 us
    all_to_all x1, waiting for transfers between devices, shards(): lax.all_to_all(send_back, 'expert', split_axis=0, concat_axis=0, tiled=True)  23.9 us
    all_gather x1, waiting for transfers between devices, shards(): lax.all_gather(w_down, 'dp', axis=1, tiled=True)  13.3 us
    all_to_all x1, starting transfers between devices, shards(): lax.all_to_all(send_in, 'expert', split_axis=0, concat_axis=0, tiled=True)  10.9 us
    all_to_all x1, starting transfers between devices, shards(): lax.all_to_all(grad_send, 'expert', split_axis=0, concat_axis=0, tiled=True)  9.98 us
    all_gather x1, waiting for transfers between devices, shards(): lax.all_gather(w_up, 'dp', axis=1, tiled=True)  9.29 us
  transfers between devices with their start and end apart: 7, of which 6 were waited for; matrix products, arithmetic and copies ran while one was open for 14% of the time, Pallas kernels for 0%

commit v1 on v0

v1 whole, which is shorter than its diff:
```python
import functools

import jax
import jax.numpy as jnp
from jax import lax
from jax.experimental import pallas as pl
from jax.experimental.pallas import tpu as pltpu
from jax.sharding import PartitionSpec as P

MESH = pl.DeviceIdType.MESH
NX, NY, NZ = 4, 4, 8
CAP = 12
CHUNKS = 4
NT = (((1,), (1,)), ((), ()))
BF = jnp.bfloat16
F32 = jnp.float32


def mm(a, b):
    return jnp.dot(a, b, preferred_element_type=F32)


def mm_nt(a, b):
    return lax.dot_general(a, b, NT, preferred_element_type=F32)


def kernel(
    tok_ref, cot_ref, meta_ref, wg_ref, wu_ref, wd_ref, out_a, out_b,
    w, t, meta, sel, comb, xs, rows, hid, acc, ys, yr, part, rsend, rrecv,
    ssem, rsem, lsem,
):
    dp, ex = lax.axis_index("dp"), lax.axis_index("expert")
    y, c = dp // 2, lax.rem(dp, 2)
    x, z = ex // NZ, lax.rem(ex, NZ)
    tok_rows, width = tok_ref.shape
    unit = wg_ref.shape[0]
    half = unit // 2
    seg = NZ * CAP
    cw = width // CHUNKS

    def at_y(step):
        return {"dp": lax.rem(y + step + NY, NY) * 2 + c, "expert": ex}

    def at_x(step):
        return {"dp": dp, "expert": lax.rem(x + step, NX) * NZ + z}

    def at_z(step):
        return {"dp": dp, "expert": x * NZ + lax.rem(z + step + NZ, NZ)}

    other = {"dp": y * 2 + 1 - c, "expert": ex}
    y_up, y_down = at_y(1), at_y(-1)
    z_up, z_down = at_z(1), at_z(-1)
    x_peers = [None] + [at_x(d) for d in range(1, NX)]

    barrier = pltpu.get_barrier_semaphore()
    greeted = [other, y_up, y_down, z_up, z_down] + x_peers[1:]
    for dev in greeted:
        pl.semaphore_signal(barrier, inc=1, device_id=dev, device_id_type=MESH)
    pl.semaphore_wait(barrier, len(greeted))

    copies = []

    def send(src, dst, dev):
        i = len(copies)
        copy = pltpu.make_async_remote_copy(
            src_ref=src, dst_ref=dst, send_sem=ssem.at[i], recv_sem=rsem.at[i],
            device_id=dev, device_id_type=MESH,
        )
        copies.append(copy)
        copy.start()
        return copy

    def zrows(step):
        return pl.ds(pl.multiple_of(lax.rem(z + step + NZ, NZ) * tok_rows, tok_rows), tok_rows)

    own = [tok_ref, cot_ref]
    ring = {}
    for a in (0, 1):
        ring[a, 1] = send(own[a], t.at[a, zrows(0)], z_up)
        ring[a, -1] = send(own[a], t.at[a, zrows(0)], z_down)
        if a == 0:
            ring[2, 1] = send(meta_ref, meta.at[z], z_up)
            ring[2, -1] = send(meta_ref, meta.at[z], z_down)

    mats = [wg_ref, wu_ref, wd_ref]

    def wrows(place, side, h):
        return pl.ds((place * 2 + side) * unit + h * half, half)

    wcopy = {}
    for m in range(3):
        for h in (0, 1):
            src = mats[m].at[pl.ds(h * half, half)]
            wcopy[m, 0, h] = send(src, w.at[m, wrows(0, 1, h)], other)
            g = 1 - h
            src_g = mats[m].at[pl.ds(g * half, half)]
            wcopy[m, 2, h] = send(src, w.at[m, wrows(2, 0, h)], y_up)
            wcopy[m, 1, g] = send(src_g, w.at[m, wrows(1, 0, g)], y_down)
    local = []
    for i, (src, dst) in enumerate(
        [(tok_ref, t.at[0, zrows(0)]), (cot_ref, t.at[1, zrows(0)]), (meta_ref, meta.at[z])]
        + [(mats[m], w.at[m, pl.ds(0, unit)]) for m in range(3)]
    ):
        copy = pltpu.make_async_copy(src, dst, lsem.at[i])
        copy.start()
        local.append(copy)

    wfwd = {}

    def forward_weights(m):
        for h in (0, 1):
            g = 1 - h
            wcopy[m, 2, h].wait_recv()
            if h == 0:
                wcopy[m, 3, 0] = send(w.at[m, wrows(2, 0, 0)], w.at[m, wrows(3, 0, 0)], y_up)
            wfwd[m, 2, h] = send(w.at[m, wrows(2, 0, h)], w.at[m, wrows(2, 1, h)], other)
            wcopy[m, 1, g].wait_recv()
            if g == 1:
                wcopy[m, 3, 1] = send(w.at[m, wrows(1, 0, 1)], w.at[m, wrows(3, 0, 1)], y_down)
            wfwd[m, 1, g] = send(w.at[m, wrows(1, 0, g)], w.at[m, wrows(1, 1, g)], other)

    def forward_last(m):
        for h in (0, 1):
            wcopy[m, 3, h].wait_recv()
            wfwd[m, 3, h] = send(w.at[m, wrows(3, 0, h)], w.at[m, wrows(3, 1, h)], other)

    hops = {(0, 1): 4, (0, -1): 3, (1, 1): 3, (1, -1): 4, (2, 1): 4, (2, -1): 3}

    def ring_step(a, step):
        for sign in (1, -1):
            if step <= hops[a, sign]:
                ring[a, sign].wait_recv()
                if step < hops[a, sign]:
                    dev = z_up if sign == 1 else z_down
                    if a == 2:
                        place = meta.at[lax.rem(z - sign * step + NZ, NZ)]
                    else:
                        place = t.at[a, zrows(-sign * step)]
                    ring[a, sign] = send(place, place, dev)

    for step in (1, 2, 3, 4):
        for a in (2, 0, 1):
            if (a, step) != (1, 4):
                ring_step(a, step)
        if step == 2:
            forward_weights(0)
    for copy in local[:3]:
        copy.wait()

    table = meta[0]
    for i in range(1, NZ):
        table = table + meta[i]
    count = NZ * tok_rows
    lane_of = lax.broadcasted_iota(jnp.int32, (count, count), 1)
    line_of = lax.broadcasted_iota(jnp.int32, (count, count), 0)
    before = ((lane_of >> 5) == (line_of >> 5)) & (line_of < lane_of)
    before = jnp.where(before, 1.0, 0.0).astype(BF)
    line8 = lax.broadcasted_iota(jnp.int32, (8, count), 0)
    base8 = ((lax.broadcasted_iota(jnp.int32, (8, count), 1) >> 5) * CAP).astype(F32)
    taken = jnp.zeros((8, count), F32)
    gates = []
    for d in range(NX):
        number = (lax.rem(x + d, NX) * NZ + z + 1).astype(F32)
        hit = jnp.where(table[0:8] == number, 1.0, 0.0)
        taken = jnp.where(line8 == d, jnp.sum(hit, axis=0, keepdims=True), taken)
        gates.append(jnp.sum(hit * table[8:16], axis=0, keepdims=True))
    place = base8 + mm(taken.astype(BF), before)
    place = jnp.where(taken > 0.5, place, -1.0)
    line_seg = lax.broadcasted_iota(jnp.int32, (seg, count), 0).astype(F32)
    weighted = []
    for d in range(NX):
        one = jnp.where(line_seg == place[d : d + 1], 1.0, 0.0)
        sel[pl.ds(d * seg, seg), :] = one.astype(BF)
        weighted.append(one * gates[d])
    weighted = jnp.concatenate(weighted, axis=0).T
    high = weighted.astype(BF)
    comb[0] = high
    comb[1] = (weighted - high.astype(F32)).astype(BF)

    xcopy = {}

    def pick(a):
        @pl.loop(0, 4)
        def _(i):
            cols = pl.ds(pl.multiple_of(i * (width // 4), width // 4), width // 4)
            got = mm(sel[...], t[a, :, cols]).astype(BF)
            rows[a, pl.ds(0, seg), cols] = got[0:seg]
            for d in range(1, NX):
                xs[a, d - 1, :, cols] = got[d * seg : (d + 1) * seg]

        for d in (2, 1, 3):
            xcopy[a, d] = send(xs.at[a, d - 1], rows.at[a, pl.ds((NX - d) * seg, seg)], x_peers[d])

    pick(0)
    ring_step(1, 4)
    pick(1)
    forward_weights(1)

    def first(row0, tiles, tile):
        @pl.loop(0, tiles)
        def _(i):
            span = pl.ds(pl.multiple_of(row0 + i * tile, 128), tile)
            into = pl.ds(pl.multiple_of(i * tile, 128), tile)
            gate = mm_nt(rows[0], w[0, span, :])
            up = mm_nt(rows[0], w[1, span, :])
            back = mm_nt(rows[1], w[2, span, :])
            sig = jax.nn.sigmoid(gate)
            silu = gate * sig
            hid[0, :, into] = (silu * up).astype(BF)
            hid[1, :, into] = (back * up * sig * (1.0 + gate * (1.0 - sig))).astype(BF)
            hid[2, :, into] = (back * silu).astype(BF)

    def second(row0, span, cols):
        both = pl.ds(row0, span)
        some = pl.ds(0, span)
        out = mm(hid[0, :, some], w[2, both, cols])
        grad = mm(hid[1, :, some], w[0, both, cols]) + mm(hid[2, :, some], w[1, both, cols])
        return out, grad

    pair = 2 * unit
    for d in range(1, NX):
        xcopy[0, d].wait_recv()
    forward_weights(2)
    for d in range(1, NX):
        xcopy[1, d].wait_recv()
    for m in range(3):
        local[3 + m].wait()
        for h in (0, 1):
            wcopy[m, 0, h].wait_recv()
    first(0, 1, pair)

    @pl.loop(0, 4)
    def _(i):
        cols = pl.ds(pl.multiple_of(i * (width // 4), width // 4), width // 4)
        out, grad = second(0, pair, cols)
        acc[0, :, cols] = out
        acc[1, :, cols] = grad

    forward_last(0)
    for m in range(3):
        for p in (1, 2):
            for h in (0, 1):
                wfwd[m, p, h].wait_recv()
    first(pair, 3, 256)
    forward_last(1)

    @pl.loop(0, 4)
    def _(i):
        cols = pl.ds(pl.multiple_of(i * (width // 4), width // 4), width // 4)
        out, grad = second(pair, 2 * pair, cols)
        acc[0, :, cols] += out
        acc[1, :, cols] += grad

    forward_last(2)
    for m in range(3):
        for h in (0, 1):
            wfwd[m, 3, h].wait_recv()
    first(3 * pair, 1, pair)

    ycopy = {}
    for j in range(CHUNKS):
        cols = pl.ds(j * cw, cw)
        for a, add in enumerate(second(3 * pair, pair, cols)):
            done = (acc[a, :, cols] + add).astype(BF)
            yr[j, a, pl.ds(0, seg), :] = done[0:seg]
            for d in (2, 1, 3):
                ys[j, a, d - 1] = done[d * seg : (d + 1) * seg]
                ycopy[j, a, d] = send(
                    ys.at[j, a, d - 1], yr.at[j, a, pl.ds((NX - d) * seg, seg)], x_peers[d]
                )

    outs = [out_a, out_b]
    for j in range(CHUNKS):
        for a in (0, 1):
            for d in range(1, NX):
                ycopy[j, a, d].wait_recv()
            part[a] = mm(comb[0], yr[j, a]) + mm(comb[1], yr[j, a])
        chain = {}
        for step in (1, 2, 3, 4):
            for a in (0, 1):
                for k, sign in enumerate((1, -1)):
                    far = hops[a, sign]
                    if step > far:
                        continue
                    term = part[a, zrows(sign * (far - step + 1)), :]
                    if step > 1:
                        chain[a, k].wait_recv()
                        term = term + rrecv[j, a, k, step - 2].astype(F32)
                    rsend[j, a, k, step - 1] = term.astype(BF)
                    chain[a, k] = send(
                        rsend.at[j, a, k, step - 1], rrecv.at[j, a, k, step - 1],
                        z_up if sign == 1 else z_down,
                    )
        for a in (0, 1):
            total = part[a, zrows(0), :]
            for k, sign in enumerate((1, -1)):
                chain[a, k].wait_recv()
                total = total + rrecv[j, a, k, hops[a, sign] - 1].astype(F32)
            outs[a][:, pl.ds(j * cw, cw)] = total.astype(BF)

    for copy in copies:
        copy.wait_send()


def shards(tokens, expert_ids, gate_weights, cotangent, w_gate, w_up, w_down):
    tok_rows, width = tokens.shape
    unit = w_gate.shape[1]
    z = lax.rem(lax.axis_index("expert"), NZ)
    meta = jnp.concatenate([expert_ids.T.astype(F32) + 1.0, gate_weights.T], axis=0)
    lane = lax.broadcasted_iota(jnp.int32, (16, NZ * tok_rows), 1)
    meta = jnp.where(lane // tok_rows == z, jnp.tile(meta, (1, NZ)), 0.0)
    seg = NZ * CAP
    slots = NX * seg
    hidden = NY * 2 * unit
    cw = width // CHUNKS
    n_copies = 42 + 21 + 6 + CHUNKS * (6 + 14)
    hbm = pl.BlockSpec(memory_space=pl.ANY)
    vmem = pl.BlockSpec(memory_space=pltpu.VMEM)
    result = jax.ShapeDtypeStruct((tok_rows, width), BF)
    return pl.pallas_call(
        kernel,
        out_shape=(result, result),
        in_specs=[hbm] * 6,
        out_specs=(vmem, vmem),
        scratch_shapes=[
            pltpu.VMEM((3, hidden, width), BF),
            pltpu.VMEM((2, NZ * tok_rows, width), BF),
            pltpu.VMEM((NZ, 16, NZ * tok_rows), F32),
            pltpu.VMEM((slots, NZ * tok_rows), BF),
            pltpu.VMEM((2, NZ * tok_rows, slots), BF),
            pltpu.VMEM((2, NX - 1, seg, width), BF),
            pltpu.VMEM((2, slots, width), BF),
            pltpu.VMEM((3, slots, 4 * unit), BF),
            pltpu.VMEM((2, slots, width), F32),
            pltpu.VMEM((CHUNKS, 2, NX - 1, seg, cw), BF),
            pltpu.VMEM((CHUNKS, 2, slots, cw), BF),
            pltpu.VMEM((2, NZ * tok_rows, cw), F32),
            pltpu.VMEM((CHUNKS, 2, 2, 4, tok_rows, cw), BF),
            pltpu.VMEM((CHUNKS, 2, 2, 4, tok_rows, cw), BF),
            pltpu.SemaphoreType.DMA((n_copies,)),
            pltpu.SemaphoreType.DMA((n_copies,)),
            pltpu.SemaphoreType.DMA((6,)),
        ],
        compiler_params=pltpu.CompilerParams(
            collective_id=0, has_side_effects=True, vmem_limit_bytes=60 * 1024 * 1024
        ),
    )(tokens, cotangent, meta, w_gate[0], w_up[0], w_down[0])


def solution(mesh):
    both = P(("dp", "expert"), None)
    weights = P("expert", "dp", None)
    return jax.shard_map(
        shards,
        mesh=mesh,
        in_specs=(both, both, both, both, weights, weights, weights),
        out_specs=(both, both),
        check_vma=False,
    )
```

time: 294 us -> 168 us (0.57)
  waiting for transfers between devices: 182 us -> 0 us
  Pallas kernels: 0 us -> 162 us
  matrix products: 38.4 us -> 0 us
  starting transfers between devices: 33.6 us -> 0 us
  local copies, waits for them, and re-layouts: 24.1 us -> 3.69 us
  between operations: 14.1 us -> 0.68 us
    pallas_call x0 -> x1, Pallas kernels: none -> 162 us  [shards(): pl.pallas_call(kernel, out_shape=(result, result), in_specs=[hbm] * 6, ou...]
    all_to_all x4 -> x0, waiting for transfers between devices: 157 us -> none  [the longest x1 46.1 us: shards(): lax.all_to_all(out_send, 'expert', split_axis=0, concat_axis=0, tiled=True)]
    dot_general x8 -> x0, matrix products: 38.4 us -> none  [the longest x1 8.33 us: expert_terms(): jnp.einsum('secd,ehd->sech', rows_in, gate_mat, preferred_element_type=jn...]
    all_to_all x4 -> x0, starting transfers between devices: 33.5 us -> none  [the longest x1 10.9 us: shards(): lax.all_to_all(send_in, 'expert', split_axis=0, concat_axis=0, tiled=True)]
    all_gather x3 -> x0, waiting for transfers between devices: 22.7 us -> none  [the longest x1 13.3 us: shards(): lax.all_gather(w_down, 'dp', axis=1, tiled=True)]
    gather x4 -> x0, local copies, waits for them, and re-layouts: 8.6 us -> none  [the longest x1 2.45 us: shards(): padded_in[slot_owner].reshape(expert_devs, local_count * capacity, width)]
    reshape x4 -> x0, local copies, waits for them, and re-layouts: 8.04 us -> none  [the longest x1 2.5 us: shards(): picked_grad = back_grad.reshape(experts_all * capacity, width)[slot_index]]
    convert_element_type x3 -> x0, local copies, waits for them, and re-layouts: 5.31 us -> none  [the longest x1 2.23 us: shards(): out_sum.astype(jnp.bfloat16)]
  transfers between devices with their start and end apart: 7 -> 0, of which waited for: 6 -> 0; matrix products, arithmetic and copies ran while one was open for 14% -> 0% of each run, Pallas kernels for 0% -> 0%
where the time goes in v1:
time: 168 us; the launch traced here: 167 us
  Pallas kernels  162 us (96%)
  local copies, waits for them, and re-layouts  3.69 us (2%)
    pallas_call x1, Pallas kernels, shards(): pl.pallas_call(kernel, out_shape=(result, result), in_specs=[hbm] * 6, ou...  162 us
    unnamed x8, local copies, waits for them, and re-layouts  3.6 us

profile of v1, /device:TPU:64, one launch (start us, length us, event | category | flops | bytes accessed | tf_op | source)
XLA Modules:
  0.0 166.9 jit_solution(3586113975474094912)
XLA Ops:
  0.6 0.0 copy-start.1
  0.7 0.7 copy-done.1
  1.3 0.0 copy-start.2
  1.3 0.7 copy-done.2
  2.0 0.1 tile.10
  2.1 0.6 fusion.meta_ref
  2.7 161.9 %shard_map.86 = (bf16[32,2048]{1,0:T(8,128)(2,1)}, bf16[32,2048]{1,0:T(8,128)(2,1)}) custom-call(bf16[32,2048]{1,0:T(8,128)(2,1)} %tok_ref.1, bf16[32,2048]{1,0:T(8,128)(2,1)} %cot_ref.1, f32[16,256]{1,0:T(8,128)} %fusion.meta_ref, bf16[192,2048]{1,0:T(8,128)(2,1)} %bitcast.6, bf16[192,2048]{1,0:T(8,128)(2,1)} %bitcast.7, bf16[192,2048]{1,0:T(8,128)(2,1)} %bitcast.8), custom_call_target="tpu_custom_call" | custom-call | tf_op jit(solution)/shard_map/pallas_call | solution.py:320
  164.7 0.0 copy-start
  164.7 1.6 copy.11
  166.3 0.0 copy-done
  166.3 0.7 copy.12
  (5 shorter events, 0.0 us)
Async XLA Ops:
  0.6 0.7 copy-start.1
  1.3 0.7 copy-start.2
  164.7 1.6 copy-start

commit v2 on v1

v2 whole, which is shorter than its diff:
```python
import functools

import jax
import jax.numpy as jnp
from jax import lax
from jax.experimental import pallas as pl
from jax.experimental.pallas import tpu as pltpu
from jax.sharding import PartitionSpec as P

MESH = pl.DeviceIdType.MESH
NX, NY, NZ = 4, 4, 8
CAP = 12
CHUNKS = 4
NT = (((1,), (1,)), ((), ()))
BF = jnp.bfloat16
F32 = jnp.float32


def mm(a, b):
    return jnp.dot(a, b, preferred_element_type=F32)


def mm_nt(a, b):
    return lax.dot_general(a, b, NT, preferred_element_type=F32)


def kernel(
    tok_ref, cot_ref, meta_ref, wg_ref, wu_ref, wd_ref, out_a, out_b,
    w, wd, t, meta, sel, comb, xs, rows, hid, fac, back, grads, ys, yr, part, rsend, rrecv,
    ssem, rsem, lsem,
):
    dp, ex = lax.axis_index("dp"), lax.axis_index("expert")
    y, c = dp // 2, lax.rem(dp, 2)
    x, z = ex // NZ, lax.rem(ex, NZ)
    tok_rows, width = tok_ref.shape
    unit = wg_ref.shape[0]
    half = unit // 2
    seg = NZ * CAP
    cw = width // CHUNKS
    hidden = 2 * NY * unit

    def at_y(step):
        return {"dp": lax.rem(y + step + NY, NY) * 2 + c, "expert": ex}

    def at_x(step):
        return {"dp": dp, "expert": lax.rem(x + step, NX) * NZ + z}

    def at_z(step):
        return {"dp": dp, "expert": x * NZ + lax.rem(z + step + NZ, NZ)}

    other = {"dp": y * 2 + 1 - c, "expert": ex}
    y_up, y_down = at_y(1), at_y(-1)
    z_dev = {1: at_z(1), -1: at_z(-1)}
    x_peers = [None] + [at_x(d) for d in range(1, NX)]

    barrier = pltpu.get_barrier_semaphore()
    greeted = [other, y_up, y_down, z_dev[1], z_dev[-1]] + x_peers[1:]
    for dev in greeted:
        pl.semaphore_signal(barrier, inc=1, device_id=dev, device_id_type=MESH)
    pl.semaphore_wait(barrier, len(greeted))

    copies = []

    def send(src, dst, dev):
        i = len(copies)
        copy = pltpu.make_async_remote_copy(
            src_ref=src, dst_ref=dst, send_sem=ssem.at[i], recv_sem=rsem.at[i],
            device_id=dev, device_id_type=MESH,
        )
        copies.append(copy)
        copy.start()
        return copy

    def zrows(step):
        return pl.ds(pl.multiple_of(lax.rem(z + step + NZ, NZ) * tok_rows, tok_rows), tok_rows)

    own = [tok_ref, cot_ref, meta_ref]
    hops = {(0, 1): 4, (0, -1): 3, (1, 1): 3, (1, -1): 4, (2, 1): 4, (2, -1): 3}
    ring = {}

    def zplace(a, step):
        if a == 2:
            return meta.at[lax.rem(z + step + NZ, NZ)]
        return t.at[a, zrows(step)]

    def ring_start(a):
        for sign in (1, -1):
            ring[a, sign] = send(own[a], zplace(a, 0), z_dev[sign])

    def ring_step(a, step):
        for sign in (1, -1):
            if step <= hops[a, sign]:
                ring[a, sign].wait_recv()
                if step < hops[a, sign]:
                    place = zplace(a, -sign * step)
                    ring[a, sign] = send(place, place, z_dev[sign])

    mats = [wg_ref, wu_ref, wd_ref]

    def wrows(place, side, h=None):
        if h is None:
            return pl.ds((place * 2 + side) * unit, unit)
        return pl.ds((place * 2 + side) * unit + h * half, half)

    wcopy, wfwd = {}, {}

    def issue(k):
        if k < 4:
            m, h = k // 2, k % 2
            g = 1 - h
            wcopy[m, 2, h] = send(mats[m].at[pl.ds(h * half, half)], w.at[m, wrows(2, 0, h)], y_up)
            wcopy[m, 1, g] = send(mats[m].at[pl.ds(g * half, half)], w.at[m, wrows(1, 0, g)], y_down)
        elif k < 6:
            m = k - 4
            wcopy[m, 3, 0] = send(w.at[m, wrows(2, 0, 0)], w.at[m, wrows(3, 0, 0)], y_up)
            wcopy[m, 3, 1] = send(w.at[m, wrows(1, 0, 1)], w.at[m, wrows(3, 0, 1)], y_down)
        elif k < 6 + CHUNKS:
            j = k - 6
            src = wd_ref.at[:, pl.ds(j * cw, cw)]
            wcopy[2, 2, j] = send(src, wd.at[j, wrows(2, 0)], y_up)
            wcopy[2, 1, j] = send(src, wd.at[j, wrows(1, 0)], y_down)

    def hand_over(m, p, h):
        wcopy[m, p, h].wait_recv()
        ref = w.at[m, wrows(p, 0, h)]
        wfwd[m, p, h] = send(ref, w.at[m, wrows(p, 1, h)], other)

    def event(k):
        if k < 4:
            m, h = k // 2, k % 2
            hand_over(m, 2, h)
            hand_over(m, 1, 1 - h)
        else:
            for h in (0, 1):
                hand_over(k - 4, 3, h)
        issue(k + 3)

    def event_down(j):
        for p, to, h, dev in ((2, 3, 0, y_up), (1, 3, 1, y_down)):
            wcopy[2, p, j].wait_recv()
            wcopy[2, 3, j, h] = send(wd.at[j, wrows(p, 0, h)], wd.at[j, wrows(3, 0, h)], dev)
            wfwd[2, p, j] = send(wd.at[j, wrows(p, 0)], wd.at[j, wrows(p, 1)], other)
        issue(9 + j)

    def event_last(j):
        for h in (0, 1):
            wcopy[2, 3, j, h].wait_recv()
            wfwd[2, 3, j, h] = send(wd.at[j, wrows(3, 0, h)], wd.at[j, wrows(3, 1, h)], other)

    ring_start(2)
    ring_start(0)
    for k in range(3):
        issue(k)
    local = []

    def local_copy(src, dst):
        copy = pltpu.make_async_copy(src, dst, lsem.at[len(local)])
        copy.start()
        local.append(copy)

    for a in range(3):
        local_copy(own[a], zplace(a, 0))
    for m in (0, 1):
        local_copy(mats[m], w.at[m, wrows(0, 0)])
        wfwd[m, 0] = send(mats[m], w.at[m, wrows(0, 1)], other)
    for j in range(CHUNKS):
        src = wd_ref.at[:, pl.ds(j * cw, cw)]
        local_copy(src, wd.at[j, wrows(0, 0)])
        wfwd[2, 0, j] = send(src, wd.at[j, wrows(0, 1)], other)

    ring_step(2, 1)
    ring_step(0, 1)
    ring_start(1)
    ring_step(2, 2)
    ring_step(0, 2)
    ring_step(1, 1)
    event(0)
    ring_step(2, 3)
    ring_step(0, 3)
    ring_step(1, 2)
    ring_step(2, 4)
    ring_step(0, 4)
    for copy in local[:3]:
        copy.wait()

    table = meta[0]
    for i in range(1, NZ):
        table = table + meta[i]
    count = NZ * tok_rows
    lane_of = lax.broadcasted_iota(jnp.int32, (count, count), 1)
    line_of = lax.broadcasted_iota(jnp.int32, (count, count), 0)
    before = ((lane_of >> 5) == (line_of >> 5)) & (line_of < lane_of)
    before = jnp.where(before, 1.0, 0.0).astype(BF)
    line8 = lax.broadcasted_iota(jnp.int32, (8, count), 0)
    base8 = ((lax.broadcasted_iota(jnp.int32, (8, count), 1) >> 5) * CAP).astype(F32)
    taken = jnp.zeros((8, count), F32)
    gates = []
    for d in range(NX):
        number = (lax.rem(x + d, NX) * NZ + z + 1).astype(F32)
        hit = jnp.where(table[0:8] == number, 1.0, 0.0)
        taken = jnp.where(line8 == d, jnp.sum(hit, axis=0, keepdims=True), taken)
        gates.append(jnp.sum(hit * table[8:16], axis=0, keepdims=True))
    place = base8 + mm(taken.astype(BF), before)
    place = jnp.where(taken > 0.5, place, -1.0)
    line_seg = lax.broadcasted_iota(jnp.int32, (seg, count), 0).astype(F32)
    weighted = []
    for d in range(NX):
        one = jnp.where(line_seg == place[d : d + 1], 1.0, 0.0)
        sel[pl.ds(d * seg, seg), :] = one.astype(BF)
        weighted.append(one * gates[d])

    xcopy = {}

    def pick(a):
        @pl.loop(0, 4)
        def _(i):
            cols = pl.ds(pl.multiple_of(i * (width // 4), width // 4), width // 4)
            got = mm(sel[...], t[a, :, cols]).astype(BF)
            rows[a, pl.ds(0, seg), cols] = got[0:seg]
            for d in range(1, NX):
                xs[a, d - 1, :, cols] = got[d * seg : (d + 1) * seg]

    def send_rows(a):
        for d in (2, 1, 3):
            xcopy[a, d] = send(xs.at[a, d - 1], rows.at[a, pl.ds((NX - d) * seg, seg)], x_peers[d])

    pick(0)
    send_rows(0)
    event(1)
    ring_step(1, 3)
    weighted = jnp.concatenate(weighted, axis=0).T
    high = weighted.astype(BF)
    comb[0] = high
    comb[1] = (weighted - high.astype(F32)).astype(BF)
    ring_step(1, 4)
    event(2)
    pick(1)
    event(3)
    for d in range(1, NX):
        xcopy[0, d].wait_recv()
    send_rows(1)

    def first(row0, tiles, tile):
        @pl.loop(0, tiles)
        def _(i):
            span = pl.ds(pl.multiple_of(row0 + i * tile, 128), tile)
            gate = mm_nt(rows[0], w[0, span, :])
            up = mm_nt(rows[0], w[1, span, :])
            sig = jax.nn.sigmoid(gate)
            silu = gate * sig
            hid[:, span] = (silu * up).astype(BF)
            fac[0, :, span] = up * sig * (1.0 + gate * (1.0 - sig))
            fac[1, :, span] = silu

    pair = 2 * unit
    for m in (0, 1):
        local[3 + m].wait()
        wfwd[m, 0].wait_recv()
    first(0, 1, pair)
    event(4)
    for m in (0, 1):
        for p in (1, 2):
            for h in (0, 1):
                wfwd[m, p, h].wait_recv()
    first(pair, 3, 256)
    event(5)
    for m in (0, 1):
        for h in (0, 1):
            wfwd[m, 3, h].wait_recv()
    first(3 * pair, 1, pair)

    ycopy, chain = {}, {}
    outs = [out_a, out_b]

    def send_back(a, j, done):
        yr[a, j, pl.ds(0, seg), :] = done[0:seg]
        for d in (2, 1, 3):
            ys[a, j, d - 1] = done[d * seg : (d + 1) * seg]
            ycopy[a, j, d] = send(
                ys.at[a, j, d - 1], yr.at[a, j, pl.ds((NX - d) * seg, seg)], x_peers[d]
            )

    def gather_back(a, j):
        for d in range(1, NX):
            ycopy[a, j, d].wait_recv()
        part[a, j] = mm(comb[0], yr[a, j]) + mm(comb[1], yr[a, j])

    def sum_step(a, j, step):
        if step == 5:
            total = part[a, j, zrows(0), :]
            for k, sign in enumerate((1, -1)):
                chain[a, j, k].wait_recv()
                total = total + rrecv[a, j, k, hops[a, sign] - 1].astype(F32)
            outs[a][:, pl.ds(j * cw, cw)] = total.astype(BF)
            return
        for k, sign in enumerate((1, -1)):
            far = hops[a, sign]
            if step > far:
                continue
            term = part[a, j, zrows(sign * (far - step + 1)), :]
            if step > 1:
                chain[a, j, k].wait_recv()
                term = term + rrecv[a, j, k, step - 2].astype(F32)
            rsend[a, j, k, step - 1] = term.astype(BF)
            chain[a, j, k] = send(
                rsend.at[a, j, k, step - 1], rrecv.at[a, j, k, step - 1], z_dev[sign]
            )

    def tick(q):
        if q < 2 * CHUNKS:
            gather_back(q // CHUNKS, q % CHUNKS)
            sum_step(q // CHUNKS, q % CHUNKS, 1)
        for i in range(1, 5):
            if 0 <= q - i < 2 * CHUNKS:
                sum_step((q - i) // CHUNKS, (q - i) % CHUNKS, 1 + i)

    def down_ready(j):
        local[5 + j].wait()
        wfwd[2, 0, j].wait_recv()
        for p in (1, 2):
            wfwd[2, p, j].wait_recv()
        for h in (0, 1):
            wfwd[2, 3, j, h].wait_recv()

    for d in range(1, NX):
        xcopy[1, d].wait_recv()
    event_down(0)
    for j in range(CHUNKS):
        if j + 1 < CHUNKS:
            event_down(j + 1)
        event_last(j)
        down_ready(j)
        send_back(0, j, mm(hid[...], wd[j]).astype(BF))

        @pl.loop(0, hidden // 256)
        def _(i):
            span = pl.ds(pl.multiple_of(i * 256, 256), 256)
            term = mm_nt(rows[1, :, pl.ds(j * cw, cw)], wd[j, span, :])
            if j > 0:
                term = term + back[:, span]
            if j + 1 < CHUNKS:
                back[:, span] = term
            else:
                grads[0, :, span] = (term * fac[0, :, span]).astype(BF)
                grads[1, :, span] = (term * fac[1, :, span]).astype(BF)

        if j > 0:
            tick(j - 1)
    for j in range(CHUNKS):
        cols = pl.ds(j * cw, cw)
        done = mm(grads[0], w[0, :, cols]) + mm(grads[1], w[1, :, cols])
        send_back(1, j, done.astype(BF))
        if j > 0:
            tick(CHUNKS + j - 2)
    for q in range(2 * CHUNKS - 2, 2 * CHUNKS + 4):
        tick(q)

    for copy in copies:
        copy.wait_send()


def shards(tokens, expert_ids, gate_weights, cotangent, w_gate, w_up, w_down):
    tok_rows, width = tokens.shape
    unit = w_gate.shape[1]
    z = lax.rem(lax.axis_index("expert"), NZ)
    meta = jnp.concatenate([expert_ids.T.astype(F32) + 1.0, gate_weights.T], axis=0)
    lane = lax.broadcasted_iota(jnp.int32, (16, NZ * tok_rows), 1)
    meta = jnp.where(lane // tok_rows == z, jnp.tile(meta, (1, NZ)), 0.0)
    seg = NZ * CAP
    slots = NX * seg
    hidden = NY * 2 * unit
    cw = width // CHUNKS
    n_copies = 26 + 9 * CHUNKS + 21 + 6 + 2 * CHUNKS * (3 + 7)
    hbm = pl.BlockSpec(memory_space=pl.ANY)
    vmem = pl.BlockSpec(memory_space=pltpu.VMEM)
    result = jax.ShapeDtypeStruct((tok_rows, width), BF)
    return pl.pallas_call(
        kernel,
        out_shape=(result, result),
        in_specs=[hbm] * 6,
        out_specs=(vmem, vmem),
        scratch_shapes=[
            pltpu.VMEM((2, hidden, width), BF),
            pltpu.VMEM((CHUNKS, hidden, cw), BF),
            pltpu.VMEM((2, NZ * tok_rows, width), BF),
            pltpu.VMEM((NZ, 16, NZ * tok_rows), F32),
            pltpu.VMEM((slots, NZ * tok_rows), BF),
            pltpu.VMEM((2, NZ * tok_rows, slots), BF),
            pltpu.VMEM((2, NX - 1, seg, width), BF),
            pltpu.VMEM((2, slots, width), BF),
            pltpu.VMEM((slots, hidden), BF),
            pltpu.VMEM((2, slots, hidden), F32),
            pltpu.VMEM((slots, hidden), F32),
            pltpu.VMEM((2, slots, hidden), BF),
            pltpu.VMEM((2, CHUNKS, NX - 1, seg, cw), BF),
            pltpu.VMEM((2, CHUNKS, slots, cw), BF),
            pltpu.VMEM((2, CHUNKS, NZ * tok_rows, cw), F32),
            pltpu.VMEM((2, CHUNKS, 2, 4, tok_rows, cw), BF),
            pltpu.VMEM((2, CHUNKS, 2, 4, tok_rows, cw), BF),
            pltpu.SemaphoreType.DMA((n_copies,)),
            pltpu.SemaphoreType.DMA((n_copies,)),
            pltpu.SemaphoreType.DMA((5 + CHUNKS,)),
        ],
        compiler_params=pltpu.CompilerParams(
            collective_id=0, has_side_effects=True, vmem_limit_bytes=60 * 1024 * 1024
        ),
    )(tokens, cotangent, meta, w_gate[0], w_up[0], w_down[0])


def solution(mesh):
    both = P(("dp", "expert"), None)
    weights = P("expert", "dp", None)
    return jax.shard_map(
        shards,
        mesh=mesh,
        in_specs=(both, both, both, both, weights, weights, weights),
        out_specs=(both, both),
        check_vma=False,
    )
```

time: 168 us -> 139 us (0.83)
  Pallas kernels: 162 us -> 132 us
    pallas_call x1, Pallas kernels: 162 us -> 132 us  [shards(): pl.pallas_call(kernel, out_shape=(result, result), in_specs=[hbm] * 6, ou...]
where the time goes in v2:
time: 139 us; the launch traced here: 137 us
  Pallas kernels  132 us (95%)
  local copies, waits for them, and re-layouts  3.69 us (3%)
    pallas_call x1, Pallas kernels, shards(): pl.pallas_call(kernel, out_shape=(result, result), in_specs=[hbm] * 6, ou...  132 us
    unnamed x8, local copies, waits for them, and re-layouts  3.6 us

profile of v2, /device:TPU:64, one launch (start us, length us, event | category | flops | bytes accessed | tf_op | source)
XLA Modules:
  0.0 137.1 jit_solution(7663123583215109391)
XLA Ops:
  0.6 0.0 copy-start.1
  0.7 0.7 copy-done.1
  1.3 0.0 copy-start.2
  1.3 0.7 copy-done.2
  2.0 0.1 tile.10
  2.1 0.6 fusion.meta_ref
  2.7 132.1 %shard_map.86 = (bf16[32,2048]{1,0:T(8,128)(2,1)}, bf16[32,2048]{1,0:T(8,128)(2,1)}) custom-call(bf16[32,2048]{1,0:T(8,128)(2,1)} %tok_ref.1, bf16[32,2048]{1,0:T(8,128)(2,1)} %cot_ref.1, f32[16,256]{1,0:T(8,128)} %fusion.meta_ref, bf16[192,2048]{1,0:T(8,128)(2,1)} %bitcast.6, bf16[192,2048]{1,0:T(8,128)(2,1)} %bitcast.7, bf16[192,2048]{1,0:T(8,128)(2,1)} %bitcast.8), custom_call_target="tpu_custom_call" | custom-call | tf_op jit(solution)/shard_map/pallas_call | solution.py:377
  134.8 0.0 copy-start
  134.8 1.6 %copy.11 = bf16[32,2048]{1,0:T(8,128)(2,1)} copy(bf16[32,2048]{1,0:T(8,128)(2,1)} %get-tuple-element.6) | data formatting | bytes 262144
  136.4 0.0 copy-done
  136.4 0.7 copy.12
  (5 shorter events, 0.0 us)
Async XLA Ops:
  0.6 0.7 copy-start.1
  1.3 0.7 copy-start.2
  134.8 1.6 %copy-start = (bf16[32,2048]{1,0:T(8,128)(2,1)S(1)}, bf16[32,2048]{1,0:T(8,128)(2,1)}, u32[]{:S(2)}) copy-start(bf16[32,2048]{1,0:T(8,128)(2,1)} %get-tuple-element.7) | copy-start | bytes 393220

commit v3 on v2

v3 whole, which is shorter than its diff:
```python
import functools

import jax
import jax.numpy as jnp
from jax import lax
from jax.experimental import pallas as pl
from jax.experimental.pallas import tpu as pltpu
from jax.sharding import PartitionSpec as P

MESH = pl.DeviceIdType.MESH
NX, NY, NZ = 4, 4, 8
CAP = 12
COLS = 256
PARTS_A = (1, 2, 2, 2, 1)
PARTS_B = (2, 2, 2, 1, 1)
RINGED = 3
NT = (((1,), (1,)), ((), ()))
BF = jnp.bfloat16
F32 = jnp.float32


def mm(a, b):
    return jnp.dot(a, b, preferred_element_type=F32)


def mm_nt(a, b):
    return lax.dot_general(a, b, NT, preferred_element_type=F32)


def kernel(
    tok_ref, cot_ref, ids_ref, gate_ref, wg_ref, wu_ref, wd_ref, out_a, out_b,
    w, t, meta, ids_in, gates_in, sel, comb, xs, rows, hid, fac, back, grads, ys, yr, part, rsend, rrecv, dsend, drecv,
    ssem, rsem, lsem,
):
    dp, ex = lax.axis_index("dp"), lax.axis_index("expert")
    y, c = dp // 2, lax.rem(dp, 2)
    x, z = ex // NZ, lax.rem(ex, NZ)
    tok_rows, width = tok_ref.shape
    unit = wg_ref.shape[0]
    half = unit // 2
    seg = NZ * CAP
    hidden = 2 * NY * unit

    def at_y(step):
        return {"dp": lax.rem(y + step + NY, NY) * 2 + c, "expert": ex}

    def at_x(step):
        return {"dp": dp, "expert": lax.rem(x + step, NX) * NZ + z}

    def at_z(step):
        return {"dp": dp, "expert": x * NZ + lax.rem(z + step + NZ, NZ)}

    other = {"dp": y * 2 + 1 - c, "expert": ex}
    y_up, y_down = at_y(1), at_y(-1)
    z_dev = {1: at_z(1), -1: at_z(-1)}
    z_peers = [None] + [at_z(s) for s in range(1, NZ)]
    x_peers = [None] + [at_x(d) for d in range(1, NX)]

    barrier = pltpu.get_barrier_semaphore()
    greeted = [other, y_up, y_down] + z_peers[1:] + x_peers[1:]
    for dev in greeted:
        pl.semaphore_signal(barrier, inc=1, device_id=dev, device_id_type=MESH)

    local = []

    def local_copy(src, dst):
        copy = pltpu.make_async_copy(src, dst, lsem.at[len(local)])
        copy.start()
        local.append(copy)

    local_copy(ids_ref, ids_in)
    local_copy(gate_ref, gates_in)
    lanes = NZ * tok_rows
    token_lane = lax.broadcasted_iota(jnp.int32, (tok_rows, lanes), 0) + z * tok_rows
    spread = token_lane == lax.broadcasted_iota(jnp.int32, (tok_rows, lanes), 1)
    spread = jnp.where(spread, 1.0, 0.0).astype(BF)
    local[0].wait()
    local[1].wait()
    meta[z, 0:8] = mm((ids_in[...].astype(F32) + 1.0).astype(BF), spread)
    rest = gates_in[...]
    spread_gates = jnp.zeros((8, lanes), F32)
    for _ in range(3):
        piece = rest.astype(BF)
        spread_gates = spread_gates + mm(piece, spread)
        rest = rest - piece.astype(F32)
    meta[z, 8:16] = spread_gates
    pl.semaphore_wait(barrier, len(greeted))

    copies = []

    def send(src, dst, dev):
        i = len(copies)
        copy = pltpu.make_async_remote_copy(
            src_ref=src, dst_ref=dst, send_sem=ssem.at[i], recv_sem=rsem.at[i],
            device_id=dev, device_id_type=MESH,
        )
        copies.append(copy)
        copy.start()
        return copy

    def zrows(step):
        return pl.ds(pl.multiple_of(lax.rem(z + step + NZ, NZ) * tok_rows, tok_rows), tok_rows)

    own = [tok_ref, cot_ref, meta.at[z]]
    hops = {(0, 1): 4, (0, -1): 3, (1, 1): 3, (1, -1): 4, (2, 1): 4, (2, -1): 3}
    ring = {}

    def zplace(a, step):
        if a == 2:
            return meta.at[lax.rem(z + step + NZ, NZ)]
        return t.at[a, zrows(step)]

    def ring_start(a):
        for sign in (1, -1):
            ring[a, sign] = send(own[a], zplace(a, 0), z_dev[sign])

    def ring_step(a, step):
        for sign in (1, -1):
            if step <= hops[a, sign]:
                ring[a, sign].wait_recv()
                if step < hops[a, sign]:
                    place = zplace(a, -sign * step)
                    ring[a, sign] = send(place, place, z_dev[sign])

    mats = [wg_ref, wu_ref, wd_ref]

    def wrows(place, side, h=None):
        if h is None:
            return pl.ds((place * 2 + side) * unit, unit)
        return pl.ds((place * 2 + side) * unit + h * half, half)

    wcopy, wfwd = {}, {}
    dcols = [pl.ds(sum(PARTS_A[:j]) * COLS, PARTS_A[j] * COLS) for j in range(len(PARTS_A))]

    def issue(k):
        if k < 4:
            m, h = k // 2, k % 2
            g = 1 - h
            wcopy[m, 2, h] = send(mats[m].at[pl.ds(h * half, half)], w.at[m, wrows(2, 0, h)], y_up)
            wcopy[m, 1, g] = send(mats[m].at[pl.ds(g * half, half)], w.at[m, wrows(1, 0, g)], y_down)
        elif k < 6:
            m = k - 4
            wcopy[m, 3, 0] = send(w.at[m, wrows(2, 0, 0)], w.at[m, wrows(3, 0, 0)], y_up)
            wcopy[m, 3, 1] = send(w.at[m, wrows(1, 0, 1)], w.at[m, wrows(3, 0, 1)], y_down)
        elif k < 6 + len(PARTS_A):
            j = k - 6
            src = wd_ref.at[:, dcols[j]]
            wcopy[2, 2, j] = send(src, w.at[2, wrows(2, 0), dcols[j]], y_up)
            wcopy[2, 1, j] = send(src, w.at[2, wrows(1, 0), dcols[j]], y_down)

    def hand_over(m, p, h):
        wcopy[m, p, h].wait_recv()
        ref = w.at[m, wrows(p, 0, h)]
        wfwd[m, p, h] = send(ref, w.at[m, wrows(p, 1, h)], other)

    def event(k):
        if k < 4:
            m, h = k // 2, k % 2
            hand_over(m, 2, h)
            hand_over(m, 1, 1 - h)
        else:
            for h in (0, 1):
                hand_over(k - 4, 3, h)

    def event_down(j):
        for p, h, dev in ((2, 0, y_up), (1, 1, y_down)):
            wcopy[2, p, j].wait_recv()
            wcopy[2, 3, j, h] = send(
                w.at[2, wrows(p, 0, h), dcols[j]], w.at[2, wrows(3, 0, h), dcols[j]], dev
            )
        issue(8 + j)
        for p in (2, 1):
            wfwd[2, p, j] = send(w.at[2, wrows(p, 0), dcols[j]], w.at[2, wrows(p, 1), dcols[j]], other)

    def event_last(j):
        for h in (0, 1):
            wcopy[2, 3, j, h].wait_recv()
            wfwd[2, 3, j, h] = send(
                w.at[2, wrows(3, 0, h), dcols[j]], w.at[2, wrows(3, 1, h), dcols[j]], other
            )

    ring_start(2)
    ring_start(0)
    for k in range(4):
        issue(k)
    for a in (0, 1):
        local_copy(own[a], zplace(a, 0))
    for m in range(3):
        local_copy(mats[m], w.at[m, wrows(0, 0)])
        wfwd[m, 0] = send(mats[m], w.at[m, wrows(0, 1)], other)

    ring_step(2, 1)
    ring_step(0, 1)
    ring_start(1)
    ring_step(2, 2)
    ring_step(0, 2)
    ring_step(1, 1)
    ring_step(2, 3)
    ring_step(0, 3)
    ring_step(1, 2)
    ring_step(2, 4)
    ring_step(0, 4)
    for copy in local[2:4]:
        copy.wait()

    table = meta[0]
    for i in range(1, NZ):
        table = table + meta[i]
    count = NZ * tok_rows
    lane_of = lax.broadcasted_iota(jnp.int32, (count, count), 1)
    line_of = lax.broadcasted_iota(jnp.int32, (count, count), 0)
    before = ((lane_of >> 5) == (line_of >> 5)) & (line_of < lane_of)
    before = jnp.where(before, 1.0, 0.0).astype(BF)
    line8 = lax.broadcasted_iota(jnp.int32, (8, count), 0)
    base8 = ((lax.broadcasted_iota(jnp.int32, (8, count), 1) >> 5) * CAP).astype(F32)
    taken = jnp.zeros((8, count), F32)
    gates = []
    for d in range(NX):
        number = (lax.rem(x + d, NX) * NZ + z + 1).astype(F32)
        hit = jnp.where(table[0:8] == number, 1.0, 0.0)
        taken = jnp.where(line8 == d, jnp.sum(hit, axis=0, keepdims=True), taken)
        gates.append(jnp.sum(hit * table[8:16], axis=0, keepdims=True))
    place = base8 + mm(taken.astype(BF), before)
    place = jnp.where(taken > 0.5, place, -1.0)
    line_seg = lax.broadcasted_iota(jnp.int32, (seg, count), 0).astype(F32)
    weighted = []
    for d in range(NX):
        one = jnp.where(line_seg == place[d : d + 1], 1.0, 0.0)
        sel[pl.ds(d * seg, seg), :] = one.astype(BF)
        weighted.append(one * gates[d])

    xcopy = {}

    def pick(a):
        @pl.loop(0, 4)
        def _(i):
            cols = pl.ds(pl.multiple_of(i * (width // 4), width // 4), width // 4)
            got = mm(sel[...], t[a, :, cols]).astype(BF)
            rows[a, pl.ds(0, seg), cols] = got[0:seg]
            for d in range(1, NX):
                xs[a, d - 1, :, cols] = got[d * seg : (d + 1) * seg]

    def send_rows(a):
        for d in (2, 1, 3):
            xcopy[a, d] = send(xs.at[a, d - 1], rows.at[a, pl.ds((NX - d) * seg, seg)], x_peers[d])

    pick(0)
    send_rows(0)
    event(0)
    issue(4)
    event(1)
    ring_step(1, 3)
    event(2)
    for k in range(5, 8):
        issue(k)
    weighted = jnp.concatenate(weighted, axis=0).T
    high = weighted.astype(BF)
    comb[0] = high
    comb[1] = (weighted - high.astype(F32)).astype(BF)
    ring_step(1, 4)
    pick(1)
    send_rows(1)
    event(3)
    event(4)
    for d in range(1, NX):
        xcopy[0, d].wait_recv()

    def first(row0, tiles, tile):
        @pl.loop(0, tiles)
        def _(i):
            span = pl.ds(pl.multiple_of(row0 + i * tile, 128), tile)
            gate = mm_nt(rows[0], w[0, span, :])
            up = mm_nt(rows[0], w[1, span, :])
            sig = jax.nn.sigmoid(gate)
            silu = gate * sig
            hid[:, span] = (silu * up).astype(BF)
            fac[0, :, span] = up * sig * (1.0 + gate * (1.0 - sig))
            fac[1, :, span] = silu

    pair = 2 * unit
    for m in (0, 1):
        local[4 + m].wait()
        wfwd[m, 0].wait_recv()
    first(0, 1, pair)
    for m in (0, 1):
        for p in (1, 2):
            for h in (0, 1):
                wfwd[m, p, h].wait_recv()
    first(pair, 3, 256)
    event(5)
    for m in (0, 1):
        for h in (0, 1):
            wfwd[m, 3, h].wait_recv()
    first(3 * pair, 1, pair)

    chunks = []
    for a, parts in enumerate((PARTS_A, PARTS_B)):
        for i, n in enumerate(parts):
            chunks.append((a, sum(parts[:i]), n, a == 0 or i < RINGED))
    ycopy, chain = {}, {}
    outs = [out_a, out_b]

    def send_back(q, done):
        a, u, n, _ = chunks[q]
        for d in (2, 1, 3):
            for i in range(n):
                ys[a, d - 1, u + i] = done[d * seg : (d + 1) * seg, i * COLS : (i + 1) * COLS]
            ycopy[q, d] = send(
                ys.at[a, d - 1, pl.ds(u, n)],
                yr.at[a, pl.ds(u, n), pl.ds((NX - d) * seg, seg)],
                x_peers[d],
            )
        for i in range(n):
            yr[a, u + i, pl.ds(0, seg), :] = done[0:seg, i * COLS : (i + 1) * COLS]

    def gather_back(q):
        a, u, n, _ = chunks[q]
        for d in range(1, NX):
            ycopy[q, d].wait_recv()
        for i in range(u, u + n):
            part[a, i] = mm(comb[0], yr[a, i]) + mm(comb[1], yr[a, i])

    def direct_sum(q, step):
        a, u, n, _ = chunks[q]
        if step == 1:
            for s in (4, 3, 5, 2, 6, 1, 7):
                dsend[s - 1, pl.ds(u, n)] = part[a, pl.ds(u, n), zrows(s), :].astype(BF)
                chain[q, s] = send(
                    dsend.at[s - 1, pl.ds(u, n)], drecv.at[s - 1, pl.ds(u, n)], z_peers[s]
                )
            return
        for s in range(1, NZ):
            chain[q, s].wait_recv()
        for i in range(u, u + n):
            total = part[a, i, zrows(0), :]
            for s in range(1, NZ):
                total = total + drecv[s - 1, i].astype(F32)
            outs[a][:, pl.ds(i * COLS, COLS)] = total.astype(BF)

    def ring_sum(q, step):
        a, u, n, _ = chunks[q]
        if step == 5:
            for k in (0, 1):
                chain[q, k].wait_recv()
            for i in range(u, u + n):
                total = part[a, i, zrows(0), :]
                for k, sign in enumerate((1, -1)):
                    total = total + rrecv[a, k, hops[a, sign] - 1, i].astype(F32)
                outs[a][:, pl.ds(i * COLS, COLS)] = total.astype(BF)
            return
        for k, sign in enumerate((1, -1)):
            far = hops[a, sign]
            if step > far:
                continue
            some = pl.ds(u, n)
            term = part[a, some, zrows(sign * (far - step + 1)), :]
            if step > 1:
                chain[q, k].wait_recv()
                term = term + rrecv[a, k, step - 2, some].astype(F32)
            rsend[a, k, step - 1, some] = term.astype(BF)
            chain[q, k] = send(
                rsend.at[a, k, step - 1, some], rrecv.at[a, k, step - 1, some], z_dev[sign]
            )

    begun = []

    def tick(*starting):
        for q, age in begun:
            if chunks[q][3] and age <= 5:
                ring_sum(q, age)
        for q, age in begun:
            if not chunks[q][3] and age == 3:
                direct_sum(q, 2)
        begun[:] = [(q, age + 1) for q, age in begun]
        for q in starting:
            gather_back(q)
            (ring_sum if chunks[q][3] else direct_sum)(q, 1)
            begun.append((q, 2))

    def layer_chunk(j):
        if j == 0:
            local[6].wait()
            wfwd[2, 0].wait_recv()
        for p in (1, 2):
            wfwd[2, p, j].wait_recv()
        for h in (0, 1):
            wfwd[2, 3, j, h].wait_recv()
        send_back(j, mm(hid[...], w[2, :, dcols[j]]).astype(BF))

    def back_chunk(j):
        @pl.loop(0, hidden // 256)
        def _(i):
            span = pl.ds(pl.multiple_of(i * 256, 256), 256)
            term = mm_nt(rows[1, :, dcols[j]], w[2, span, dcols[j]])
            if j > 0:
                term = term + back[:, span]
            if j + 1 < len(PARTS_A):
                back[:, span] = term
            else:
                grads[0, :, span] = (term * fac[0, :, span]).astype(BF)
                grads[1, :, span] = (term * fac[1, :, span]).astype(BF)

    def grad_chunk(q):
        _, u, n, _ = chunks[q]
        cols = pl.ds(u * COLS, n * COLS)
        done = mm(grads[0], w[0, :, cols]) + mm(grads[1], w[1, :, cols])
        send_back(q, done.astype(BF))

    event_down(0)
    event_down(1)
    event_last(0)
    layer_chunk(0)
    for d in range(1, NX):
        xcopy[1, d].wait_recv()
    back_chunk(0)
    event_down(2)
    event_last(1)
    layer_chunk(1)
    back_chunk(1)
    tick(0)
    event_down(3)
    event_last(2)
    layer_chunk(2)
    event_down(4)
    back_chunk(2)
    tick(1)
    event_last(3)
    layer_chunk(3)
    event_last(4)
    back_chunk(3)
    layer_chunk(4)
    settled = len(copies)
    back_chunk(4)
    grad_chunk(5)
    grad_chunk(6)
    grad_chunk(7)
    tick(2, 3, 4)
    grad_chunk(8)
    grad_chunk(9)
    tick(5)
    for copy in copies[:settled]:
        copy.wait_send()
    tick(6)
    tick(7)
    tick(8)
    tick(9)
    tick()
    tick()

    for copy in copies[settled:]:
        copy.wait_send()


def shards(tokens, expert_ids, gate_weights, cotangent, w_gate, w_up, w_down):
    tok_rows, width = tokens.shape
    unit = w_gate.shape[1]
    seg = NZ * CAP
    slots = NX * seg
    hidden = NY * 2 * unit
    units = width // COLS
    n_copies = 27 + 8 * len(PARTS_A) + 21 + 6 + (len(PARTS_A) + len(PARTS_B)) * (3 + 7)
    hbm = pl.BlockSpec(memory_space=pl.ANY)
    vmem = pl.BlockSpec(memory_space=pltpu.VMEM)
    result = jax.ShapeDtypeStruct((tok_rows, width), BF)
    return pl.pallas_call(
        kernel,
        out_shape=(result, result),
        in_specs=[hbm] * 7,
        out_specs=(vmem, vmem),
        scratch_shapes=[
            pltpu.VMEM((3, hidden, width), BF),
            pltpu.VMEM((2, NZ * tok_rows, width), BF),
            pltpu.VMEM((NZ, 16, NZ * tok_rows), F32),
            pltpu.VMEM((8, tok_rows), jnp.int32),
            pltpu.VMEM((8, tok_rows), F32),
            pltpu.VMEM((slots, NZ * tok_rows), BF),
            pltpu.VMEM((2, NZ * tok_rows, slots), BF),
            pltpu.VMEM((2, NX - 1, seg, width), BF),
            pltpu.VMEM((2, slots, width), BF),
            pltpu.VMEM((slots, hidden), BF),
            pltpu.VMEM((2, slots, hidden), F32),
            pltpu.VMEM((slots, hidden), F32),
            pltpu.VMEM((2, slots, hidden), BF),
            pltpu.VMEM((2, NX - 1, units, seg, COLS), BF),
            pltpu.VMEM((2, units, slots, COLS), BF),
            pltpu.VMEM((2, units, NZ * tok_rows, COLS), F32),
            pltpu.VMEM((2, 2, 4, units, tok_rows, COLS), BF),
            pltpu.VMEM((2, 2, 4, units, tok_rows, COLS), BF),
            pltpu.VMEM((NZ - 1, units, tok_rows, COLS), BF),
            pltpu.VMEM((NZ - 1, units, tok_rows, COLS), BF),
            pltpu.SemaphoreType.DMA((n_copies,)),
            pltpu.SemaphoreType.DMA((n_copies,)),
            pltpu.SemaphoreType.DMA((7,)),
        ],
        compiler_params=pltpu.CompilerParams(
            collective_id=0, has_side_effects=True, vmem_limit_bytes=60 * 1024 * 1024
        ),
    )(tokens, cotangent, expert_ids.T, gate_weights.T, w_gate[0], w_up[0], w_down[0])


def solution(mesh):
    both = P(("dp", "expert"), None)
    weights = P("expert", "dp", None)
    return jax.shard_map(
        shards,
        mesh=mesh,
        in_specs=(both, both, both, both, weights, weights, weights),
        out_specs=(both, both),
        check_vma=False,
    )
```

time: 139 us -> 134 us (0.964)
  Pallas kernels: 132 us -> 130 us
  local copies, waits for them, and re-layouts: 3.69 us -> 2.26 us
    pallas_call x1, Pallas kernels: 132 us -> 130 us  [shards(): pl.pallas_call(kernel, out_shape=(result, result), in_specs=[hbm] * 7, ou...]
    unnamed x8 -> x4, local copies, waits for them, and re-layouts: 3.6 us -> 2.26 us
where the time goes in v3:
time: 134 us; the launch traced here: 133 us
  Pallas kernels  130 us (97%)
  local copies, waits for them, and re-layouts  2.26 us (2%)
    pallas_call x1, Pallas kernels, shards(): pl.pallas_call(kernel, out_shape=(result, result), in_specs=[hbm] * 7, ou...  130 us

profile of v3, /device:TPU:64, one launch (start us, length us, event | category | flops | bytes accessed | tf_op | source)
XLA Modules:
  0.0 132.8 jit_solution(17027345545321065760)
XLA Ops:
  0.6 129.9 %shard_map.86 = (bf16[32,2048]{1,0:T(8,128)(2,1)}, bf16[32,2048]{1,0:T(8,128)(2,1)}) custom-call(bf16[32,2048]{1,0:T(8,128)(2,1)} %tok_ref.1, bf16[32,2048]{1,0:T(8,128)(2,1)} %cot_ref.1, s32[8,32]{1,0:T(8,128)} %bitcast.8, f32[8,32]{1,0:T(8,128)} %bitcast.9, bf16[192,2048]{1,0:T(8,128)(2,1)} %bitcast.5, bf16[192,2048]{1,0:T(8,128)(2,1)} %bitcast.6, ...), custom_call_target="tpu_custom_call" | custom-call | tf_op jit(solution)/shard_map/pallas_call | solution.py:465
  130.6 0.0 copy-start
  130.6 1.6 %copy.11 = bf16[32,2048]{1,0:T(8,128)(2,1)} copy(bf16[32,2048]{1,0:T(8,128)(2,1)} %get-tuple-element.4) | data formatting | bytes 262144
  132.2 0.0 copy-done
  132.2 0.7 copy.12
Async XLA Ops:
  130.6 1.6 %copy-start = (bf16[32,2048]{1,0:T(8,128)(2,1)S(1)}, bf16[32,2048]{1,0:T(8,128)(2,1)}, u32[]{:S(2)}) copy-start(bf16[32,2048]{1,0:T(8,128)(2,1)} %get-tuple-element.5) | copy-start | bytes 393220

commit v4 on v3

--- a/solution.py
+++ b/solution.py
@@ -443,11 +443,14 @@
     tick(6)
     tick(7)
     tick(8)
+    later = len(copies)
+    for copy in copies[settled:later]:
+        copy.wait_send()
     tick(9)
     tick()
     tick()
 
-    for copy in copies[settled:]:
+    for copy in copies[later:]:
         copy.wait_send()
 
 
@@ -461,7 +464,7 @@
     n_copies = 27 + 8 * len(PARTS_A) + 21 + 6 + (len(PARTS_A) + len(PARTS_B)) * (3 + 7)
     hbm = pl.BlockSpec(memory_space=pl.ANY)
     vmem = pl.BlockSpec(memory_space=pltpu.VMEM)
-    result = jax.ShapeDtypeStruct((tok_rows, width), BF)
+    result = pltpu.VMEM((tok_rows, width), BF)
     return pl.pallas_call(
         kernel,
         out_shape=(result, result),

time: 134 us -> 132 us (0.985)
  no operation moved by 1% of the time
where the time goes in v4:
time: 132 us; the launch traced here: 131 us
  Pallas kernels  129 us (98%)
    pallas_call x1, Pallas kernels, shards(): pl.pallas_call(kernel, out_shape=(result, result), in_specs=[hbm] * 7, ou...  129 us

profile of v4, /device:TPU:64, one launch (start us, length us, event | category | flops | bytes accessed | tf_op | source)
XLA Modules:
  0.0 131.0 jit_solution(5904194766200850715)
XLA Ops:
  0.6 129.1 %shard_map.86 = (bf16[32,2048]{1,0:T(8,128)(2,1)S(1)}, bf16[32,2048]{1,0:T(8,128)(2,1)S(1)}) custom-call(bf16[32,2048]{1,0:T(8,128)(2,1)} %tok_ref.1, bf16[32,2048]{1,0:T(8,128)(2,1)} %cot_ref.1, s32[8,32]{1,0:T(8,128)} %bitcast.8, f32[8,32]{1,0:T(8,128)} %bitcast.9, bf16[192,2048]{1,0:T(8,128)(2,1)} %bitcast.5, bf16[192,2048]{1,0:T(8,128)(2,1)} %bitcast.6, ...), custom_call_target="tpu_custom_call" | custom-call | tf_op jit(solution)/shard_map/pallas_call | solution.py:468
  129.7 0.7 copy.11
  130.4 0.7 copy.12

commit v5 on v4

--- a/solution.py
+++ b/solution.py
@@ -406,9 +406,12 @@
         done = mm(grads[0], w[0, :, cols]) + mm(grads[1], w[1, :, cols])
         send_back(q, done.astype(BF))
 
+    early = len(copies)
     event_down(0)
     event_down(1)
     event_last(0)
+    for copy in copies[:early]:
+        copy.wait_send()
     layer_chunk(0)
     for d in range(1, NX):
         xcopy[1, d].wait_recv()
@@ -434,11 +437,10 @@
     grad_chunk(5)
     grad_chunk(6)
     grad_chunk(7)
-    tick(2, 3, 4)
     grad_chunk(8)
     grad_chunk(9)
-    tick(5)
-    for copy in copies[:settled]:
+    tick(2, 3, 4, 5)
+    for copy in copies[early:settled]:
         copy.wait_send()
     tick(6)
     tick(7)

time: 132 us -> 131 us (level)
  no operation moved by 1% of the time
where the time goes in v5:
time: 131 us
  Pallas kernels  129 us (98%)
  local copies, waits for them, and re-layouts  1.31 us (1%)
    pallas_call x1, Pallas kernels, shards(): pl.pallas_call(kernel, out_shape=(result, result), in_specs=[hbm] * 7, ou...  129 us

profile of v5, /device:TPU:64, one launch (start us, length us, event | category | flops | bytes accessed | tf_op | source)
XLA Modules:
  0.0 130.7 jit_solution(16709431203110544287)
XLA Ops:
  0.6 128.7 %shard_map.86 = (bf16[32,2048]{1,0:T(8,128)(2,1)S(1)}, bf16[32,2048]{1,0:T(8,128)(2,1)S(1)}) custom-call(bf16[32,2048]{1,0:T(8,128)(2,1)} %tok_ref.1, bf16[32,2048]{1,0:T(8,128)(2,1)} %cot_ref.1, s32[8,32]{1,0:T(8,128)} %bitcast.8, f32[8,32]{1,0:T(8,128)} %bitcast.9, bf16[192,2048]{1,0:T(8,128)(2,1)} %bitcast.5, bf16[192,2048]{1,0:T(8,128)(2,1)} %bitcast.6, ...), custom_call_target="tpu_custom_call" | custom-call | tf_op jit(solution)/shard_map/pallas_call | solution.py:470
  129.4 0.7 copy.11
  130.0 0.7 copy.12
